TPU v7x, 32 devices: a whole 2x2x4 slice. The times are simulated.
32 devices in a mesh: dp: 16 (over z, y, core), seq: 2 (over x).
Axes of the slice: x: 2, y: 2, z: 4, core: 2. Of those that a mesh axis runs over, the one named last changes fastest.
Arguments:
- small_tokens: bfloat16 [32, 196, 768], P(('dp', 'seq')), may hold values from -6 to 6
- large_tokens: bfloat16 [16, 784, 768], P('dp', 'seq'), may hold values from -6 to 6
- small_counts: int32 [32], P(('dp', 'seq')), may hold values from 166 to 196, as said below
- large_counts: int32 [16], P('dp'), may hold values from 666 to 784, as said below
- small_cot: bfloat16 [32, 196, 768], P(('dp', 'seq')), may hold values from -6 to 6
- large_cot: bfloat16 [16, 784, 768], P('dp', 'seq'), may hold values from -6 to 6
- w_qkv: float32 [768, 2304], P(('dp', 'seq')), may hold values from -0.21875 to 0.21875
- w_out: float32 [768, 768], P(('dp', 'seq')), may hold values from -0.875 to 0.875
- w_up: float32 [768, 3072], P(('dp', 'seq')), may hold values from -0.21875 to 0.21875
- w_down: float32 [3072, 768], P(('dp', 'seq')), may hold values from -0.109375 to 0.109375
- norm_params: float32 [4, 768], P(None, ('dp', 'seq')), as said below
- proj_bias: float32 [4, 768], P(None, ('dp', 'seq')), may hold values from -1.8 to 1.8
- up_bias: float32 [3072], P(('dp', 'seq')), may hold values from -1.8 to 1.8
Outputs:
- small_out: bfloat16 [32, 196, 768], P(('dp', 'seq'))
- large_out: bfloat16 [16, 784, 768], P('dp', 'seq')
- small_grad: bfloat16 [32, 196, 768], P(('dp', 'seq'))
- large_grad: bfloat16 [16, 784, 768], P('dp', 'seq')
- grad_qkv: float32 [768, 2304], P(('dp', 'seq'))
- grad_out: float32 [768, 768], P(('dp', 'seq'))
- grad_up: float32 [768, 3072], P(('dp', 'seq'))
- grad_down: float32 [3072, 768], P(('dp', 'seq'))
- grad_norm: float32 [4, 768], P(None, ('dp', 'seq'))
- grad_bias: float32 [4, 768], P(None, ('dp', 'seq'))
- grad_up_bias: float32 [3072], P(('dp', 'seq'))
Inputs may be any that keep to these rules, and one draw needn't show every extreme that they name: `small_counts`: an image's kept patches fill its first slots, the others are padding; some small image keeps all 196 and some keeps the fewest. `large_counts`: an image's kept patches fill its first slots, the others are padding; some large image keeps all 784 and some keeps the fewest. `norm_params`: rows 0 and 2 are gains between 0.5 and 1.5, rows 1 and 3 shifts.
All inputs are finite; a program needn't handle non-finite values.
Results may differ from a plain program's by a relative error of at most 0.012.
The roundings to bfloat16 on the way count: a program that leaves them out, or rounds other values in their place, can miss the bound.
Values may be sent and summed in bfloat16 or wider, within the bound.
A program may use at most 192 MiB of HBM per device.

v0:
```python
import jax
import jax.numpy as jnp
from jax import lax
from jax.sharding import PartitionSpec as P

HEAD_DIM = 64


def norm_rows(values, gain, shift):
    centre = jnp.mean(values, -1, keepdims=True)
    centered = values - centre
    spread = jnp.mean(centered * centered, -1, keepdims=True)
    return centered * lax.rsqrt(spread + 1e-06) * gain + shift


def gelu_exact(values):
    return jax.nn.gelu(values, approximate=False)


def dot_rows(left, right):
    return lax.dot_general(
        left, right, (((0,), (0,)), ((), ())), preferred_element_type=jnp.float32
    )


def dot_cols(left, right):
    return lax.dot_general(
        left, right, (((1,), (1,)), ((), ())), preferred_element_type=jnp.float32
    )


def attend(query, key_part, value, valid_keys, factor):
    raw_scores = jnp.einsum("bqhe,bkhe->bhqk", query, key_part, preferred_element_type=jnp.float32)
    scaled = jnp.where(valid_keys[:, None, None, :], raw_scores * factor, -1e30)
    row_top = jnp.max(scaled, -1, keepdims=True)
    expo_rows = jnp.exp(scaled - row_top)
    totals = jnp.sum(expo_rows, -1, keepdims=True)
    probs_full = expo_rows / totals
    mixed = jnp.einsum(
        "bhqk,bkhe->bqhe",
        probs_full.astype(jnp.bfloat16),
        value,
        preferred_element_type=jnp.float32,
    )
    return (mixed, row_top + jnp.log(totals))


def attend_back(query, key_part, value, valid_keys, log_total, grad_mixed, factor):
    raw_scores = jnp.einsum("bqhe,bkhe->bhqk", query, key_part, preferred_element_type=jnp.float32)
    scaled = jnp.where(valid_keys[:, None, None, :], raw_scores * factor, -1e30)
    probs_full = jnp.exp(scaled - log_total)
    grad_value = jnp.einsum(
        "bhqk,bqhe->bkhe",
        probs_full.astype(jnp.bfloat16),
        grad_mixed,
        preferred_element_type=jnp.float32,
    )
    grad_probs = jnp.einsum(
        "bqhe,bkhe->bhqk", grad_mixed, value, preferred_element_type=jnp.float32
    )
    row_delta = jnp.sum(probs_full * grad_probs, -1, keepdims=True)
    grad_raw = (probs_full * (grad_probs - row_delta) * factor).astype(jnp.bfloat16)
    grad_query = jnp.einsum(
        "bhqk,bkhe->bqhe", grad_raw, key_part, preferred_element_type=jnp.float32
    )
    grad_key = jnp.einsum("bhqk,bqhe->bkhe", grad_raw, query, preferred_element_type=jnp.float32)
    return (grad_query, grad_key, grad_value)


def shards(
    small_tokens,
    large_tokens,
    small_counts,
    large_counts,
    small_cot,
    large_cot,
    w_qkv,
    w_out,
    w_up,
    w_down,
    norm_params,
    proj_bias,
    up_bias,
):
    gathered = (
        lax.all_gather(w_qkv.astype(jnp.bfloat16), ("dp", "seq"), axis=0, tiled=True),
        lax.all_gather(w_out.astype(jnp.bfloat16), ("dp", "seq"), axis=0, tiled=True),
        lax.all_gather(w_up.astype(jnp.bfloat16), ("dp", "seq"), axis=0, tiled=True),
        lax.all_gather(w_down.astype(jnp.bfloat16), ("dp", "seq"), axis=0, tiled=True),
        lax.all_gather(norm_params.astype(jnp.bfloat16), ("dp", "seq"), axis=1, tiled=True),
        lax.all_gather(proj_bias.astype(jnp.bfloat16), ("dp", "seq"), axis=1, tiled=True),
        lax.all_gather(up_bias.astype(jnp.bfloat16), ("dp", "seq"), axis=0, tiled=True),
    )
    full_qkv, full_out, full_up, full_down, full_norm, full_bias, full_upbias = gathered
    norm_vals = full_norm.astype(jnp.float32)
    bias_vals = full_bias.astype(jnp.float32)
    upbias_vals = full_upbias.astype(jnp.float32)
    factor = HEAD_DIM ** (-0.5)
    small_images, small_len, width_dim = small_tokens.shape
    half_len = large_tokens.shape[1]
    small_rows = small_images * small_len
    head_count = width_dim // HEAD_DIM
    rows_in = jnp.concatenate(
        [small_tokens.reshape(small_rows, width_dim), large_tokens.reshape(half_len, width_dim)]
    ).astype(jnp.float32)
    normed_one, norm_one_back = jax.vjp(norm_rows, rows_in, norm_vals[0], norm_vals[1])
    normed_one = normed_one.astype(jnp.bfloat16)
    qkv_bias = jnp.concatenate([bias_vals[0], jnp.zeros((width_dim,), jnp.float32), bias_vals[1]])
    qkv_rows = (
        jnp.dot(normed_one, full_qkv, preferred_element_type=jnp.float32) + qkv_bias
    ).astype(jnp.bfloat16)
    qkv_heads = qkv_rows.reshape(-1, 3, head_count, HEAD_DIM)
    small_heads = qkv_heads[:small_rows].reshape(small_images, small_len, 3, head_count, HEAD_DIM)
    query_small = small_heads[:, :, 0]
    key_small = small_heads[:, :, 1]
    value_small = small_heads[:, :, 2]
    valid_small = jnp.arange(small_len, dtype=jnp.int32)[None, :] < small_counts[:, None]
    large_heads = qkv_heads[small_rows:]
    query_large = large_heads[:, 0][None]
    key_whole, value_whole = (
        lax.all_gather(large_heads[:, 1], "seq", axis=0, tiled=True),
        lax.all_gather(large_heads[:, 2], "seq", axis=0, tiled=True),
    )
    key_large = key_whole[None]
    value_large = value_whole[None]
    valid_large = jnp.arange(key_whole.shape[0], dtype=jnp.int32)[None, :] < large_counts[:, None]
    mixed_small, total_small = attend(query_small, key_small, value_small, valid_small, factor)
    mixed_large, total_large = attend(query_large, key_large, value_large, valid_large, factor)
    mixed = jnp.concatenate(
        [mixed_small.reshape(small_rows, width_dim), mixed_large.reshape(half_len, width_dim)]
    ).astype(jnp.bfloat16)
    middle = rows_in + jnp.dot(mixed, full_out, preferred_element_type=jnp.float32) + bias_vals[2]
    normed_two, norm_two_back = jax.vjp(norm_rows, middle, norm_vals[2], norm_vals[3])
    normed_two = normed_two.astype(jnp.bfloat16)
    up_proj = jnp.dot(normed_two, full_up, preferred_element_type=jnp.float32) + upbias_vals
    act_full, gelu_back = jax.vjp(gelu_exact, up_proj)
    act_low = act_full.astype(jnp.bfloat16)
    result = middle + jnp.dot(act_low, full_down, preferred_element_type=jnp.float32) + bias_vals[3]
    result_low = result.astype(jnp.bfloat16)
    small_out = result_low[:small_rows].reshape(small_tokens.shape)
    large_out = result_low[small_rows:].reshape(large_tokens.shape)
    back_qkv, back_out, back_up, back_down = (full_qkv, full_out, full_up, full_down)
    grad_rows = jnp.concatenate(
        [small_cot.reshape(small_rows, width_dim), large_cot.reshape(half_len, width_dim)]
    )
    grad_rows_full = grad_rows.astype(jnp.float32)
    grad_down = dot_rows(act_low, grad_rows)
    grad_bias_down = jnp.sum(grad_rows, 0, dtype=jnp.float32)
    grad_act = dot_cols(grad_rows, back_down)
    (grad_hidden,) = gelu_back(grad_act)
    grad_hidden_low = grad_hidden.astype(jnp.bfloat16)
    grad_up = dot_rows(normed_two, grad_hidden_low)
    grad_up_bias = jnp.sum(grad_hidden_low, 0, dtype=jnp.float32)
    grad_normed_two = dot_cols(grad_hidden_low, back_up)
    grad_mid_norm, grad_gain_two, grad_shift_two = norm_two_back(grad_normed_two)
    grad_middle = grad_rows_full + grad_mid_norm
    grad_middle_low = grad_middle.astype(jnp.bfloat16)
    grad_out = dot_rows(mixed, grad_middle_low)
    grad_bias_out = jnp.sum(grad_middle_low, 0, dtype=jnp.float32)
    grad_mixed = (
        dot_cols(grad_middle_low, back_out).astype(jnp.bfloat16).reshape(-1, head_count, HEAD_DIM)
    )
    grad_mixed_small = grad_mixed[:small_rows].reshape(
        small_images, small_len, head_count, HEAD_DIM
    )
    grad_mixed_large = grad_mixed[small_rows:][None]
    gq_small, gk_small, gv_small = attend_back(
        query_small, key_small, value_small, valid_small, total_small, grad_mixed_small, factor
    )
    gq_large, gk_whole, gv_whole = attend_back(
        query_large, key_large, value_large, valid_large, total_large, grad_mixed_large, factor
    )
    gk_large, gv_large = (
        lax.psum_scatter(
            gk_whole[0].astype(jnp.bfloat16), "seq", scatter_dimension=0, tiled=True
        ).astype(jnp.float32),
        lax.psum_scatter(
            gv_whole[0].astype(jnp.bfloat16), "seq", scatter_dimension=0, tiled=True
        ).astype(jnp.float32),
    )
    grad_qkv_small = jnp.stack([gq_small, gk_small, gv_small], 2).reshape(small_rows, 3 * width_dim)
    grad_qkv_large = jnp.stack([gq_large[0], gk_large, gv_large], 1).reshape(
        half_len, 3 * width_dim
    )
    grad_qkv_low = jnp.concatenate([grad_qkv_small, grad_qkv_large]).astype(jnp.bfloat16)
    grad_qkv = dot_rows(normed_one, grad_qkv_low)
    grad_bias_query = jnp.sum(grad_qkv_low[:, :width_dim], 0, dtype=jnp.float32)
    grad_bias_value = jnp.sum(grad_qkv_low[:, 2 * width_dim :], 0, dtype=jnp.float32)
    grad_normed_one = dot_cols(grad_qkv_low, back_qkv)
    grad_in_norm, grad_gain_one, grad_shift_one = norm_one_back(grad_normed_one)
    grad_input = (grad_middle + grad_in_norm).astype(jnp.bfloat16)
    small_grad = grad_input[:small_rows].reshape(small_tokens.shape)
    large_grad = grad_input[small_rows:].reshape(large_tokens.shape)
    grad_norm_all = jnp.stack([grad_gain_one, grad_shift_one, grad_gain_two, grad_shift_two])
    grad_bias_all = jnp.stack([grad_bias_query, grad_bias_value, grad_bias_out, grad_bias_down])
    shard_qkv, shard_out, shard_up, shard_down, shard_norm, shard_bias, shard_up_bias = (
        lax.psum_scatter(grad_qkv, ("dp", "seq"), scatter_dimension=0, tiled=True),
        lax.psum_scatter(grad_out, ("dp", "seq"), scatter_dimension=0, tiled=True),
        lax.psum_scatter(grad_up, ("dp", "seq"), scatter_dimension=0, tiled=True),
        lax.psum_scatter(grad_down, ("dp", "seq"), scatter_dimension=0, tiled=True),
        lax.psum_scatter(grad_norm_all, ("dp", "seq"), scatter_dimension=1, tiled=True),
        lax.psum_scatter(grad_bias_all, ("dp", "seq"), scatter_dimension=1, tiled=True),
        lax.psum_scatter(grad_up_bias, ("dp", "seq"), scatter_dimension=0, tiled=True),
    )
    return (
        small_out,
        large_out,
        small_grad,
        large_grad,
        shard_qkv,
        shard_out,
        shard_up,
        shard_down,
        shard_norm,
        shard_bias,
        shard_up_bias,
    )


def solution(mesh):
    in_specs = (
        P(("dp", "seq"), None, None),
        P("dp", "seq", None),
        P(("dp", "seq")),
        P("dp"),
        P(("dp", "seq"), None, None),
        P("dp", "seq", None),
        P(("dp", "seq"), None),
        P(("dp", "seq"), None),
        P(("dp", "seq"), None),
        P(("dp", "seq"), None),
        P(None, ("dp", "seq")),
        P(None, ("dp", "seq")),
        P(("dp", "seq")),
    )
    out_specs = (
        P(("dp", "seq"), None, None),
        P("dp", "seq", None),
        P(("dp", "seq"), None, None),
        P("dp", "seq", None),
        P(("dp", "seq"), None),
        P(("dp", "seq"), None),
        P(("dp", "seq"), None),
        P(("dp", "seq"), None),
        P(None, ("dp", "seq")),
        P(None, ("dp", "seq")),
        P(("dp", "seq")),
    )
    return jax.shard_map(shards, mesh=mesh, in_specs=in_specs, out_specs=out_specs, check_vma=False)
```

profile of v0, /device:TPU:0, one launch (start us, length us, event | category | flops | bytes accessed | tf_op | source)
XLA Modules:
  0.0 1075.5 jit_solution(7675551926045486599)
XLA Ops:
  9.7 69.8 %all-gather.3 = bf16[32,24,4]{1,2,0:T(4,128)(2,1)S(1)} all-gather(bf16[1,24,4]{1,2,0:T(4,128)(2,1)S(1)} %convert_bitcast_fusion), channel_id=1, replica_groups=mesh['dp'=16,'seq'=2] {'dp','seq'}, dimensions={0}, use_global_device_ids=true | all-gather | bytes 6336 | tf_op jit(solution)/shard_map/all_gather | solution.py:91
  80.2 63.4 %all-gather.2 = bf16[32,24,4]{1,2,0:T(4,128)(2,1)S(1)} all-gather(bf16[1,24,4]{1,2,0:T(4,128)(2,1)S(1)} %convert_bitcast_fusion.1), channel_id=1, replica_groups=mesh['dp'=16,'seq'=2] {'dp','seq'}, dimensions={0}, use_global_device_ids=true | all-gather | bytes 6336 | tf_op jit(solution)/shard_map/all_gather | solution.py:90
  169.9 38.2 %all-reduce = bf16[3072]{0:T(1024)(128)(2,1)S(1)} all-reduce(bf16[3072]{0:T(1024)(128)(2,1)S(1)} %dynamic-update-slice), channel_id=1, replica_groups=mesh['dp'=16,'seq'=2] {'dp','seq'}, use_global_device_ids=true, to_apply=%add | all-reduce | flops 3072 | bytes 12288
  219.4 10.3 fusion.125
  229.7 25.2 %all-gather.19.cloned.1.call-done = bf16[784,1,12,64]{3,2,1,0:T(8,128)(2,1)} async-done(((bf16[392,1,12,64]{3,2,1,0:T(8,128)(2,1)}), bf16[784,1,12,64]{3,2,1,0:T(8,128)(2,1)}) %all-gather.19.cloned.1.call-update) | async-done | bytes 1204240 | tf_op jit(solution)/shard_map/all_gather | solution.py:122
  260.1 8.9 fusion.5
  270.8 5.8 fusion.63
  276.6 35.9 %all-gather.13.cloned.1.call-done = bf16[768,768]{1,0:T(8,128)(2,1)} async-done(((bf16[24,768]{1,0:T(8,128)(2,1)}), bf16[768,768]{1,0:T(8,128)(2,1)}) %all-gather.13.cloned.1.call-update) | async-done | bytes 1179664 | tf_op jit(solution)/shard_map/all_gather | solution.py:87
  317.1 61.3 %all-gather.15.cloned.1.call-done = bf16[768,3072]{1,0:T(8,128)(2,1)} async-done(((bf16[24,3072]{1,0:T(8,128)(2,1)}), bf16[768,3072]{1,0:T(8,128)(2,1)}) %all-gather.15.cloned.1.call-update) | async-done | bytes 4718608 | tf_op jit(solution)/shard_map/all_gather | solution.py:88
  378.4 23.8 %multiply_convert_fusion.1 = (bf16[588,3072]{1,0:T(8,128)(2,1)}, f32[588,3072]{1,0:T(8,128)}, f32[588,3072]{1,0:T(8,128)}) fusion(f32[3072]{0:T(1024)S(1)} %convert_element_type.142, bf16[768,3072]{1,0:T(8,128)(2,1)} %all-gather.15.cloned.1.call-done, f32[588,768]{1,0:T(8,128)} %copy-done.3, f32[768]{0:T(1024)S(1)} %get-tuple-element.24, ...), kind=kOutput, calls=%fused_computation.24 | convolution fusion | flops 2896008192 | bytes 24611424 | tf_op jit(solution)/shard_map/dot_general | solution.py:135
  402.2 42.1 %all-gather.17.cloned.1.call-done = bf16[3072,768]{1,0:T(8,128)(2,1)} async-done(((bf16[96,768]{1,0:T(8,128)(2,1)}), bf16[3072,768]{1,0:T(8,128)(2,1)}) %all-gather.17.cloned.1.call-update) | async-done | bytes 4718608 | tf_op jit(solution)/shard_map/all_gather | solution.py:89
  444.2 10.2 convert_reduce_fusion
  465.9 10.2 fusion.52
  478.6 10.1 fusion.66
  488.7 42.5 %fusion.55 = bf16[12,64,784]{2,1,0:T(8,128)(2,1)} fusion(f32[12,392,784]{2,1,0:T(8,128)} %fusion.66, f32[12,392,784]{2,1,0:T(8,128)} %get-tuple-element.41, f32[12,392]{1,0:T(8,128)S(1)} %log_add_fusion, bf16[392,3,12,64]{0,3,2,1:T(8,128)(2,1)} %bitcast.160), kind=kOutput, calls=%fused_computation.81 | convolution fusion | flops 498478976 | bytes 69492736 | tf_op jit(solution)/shard_map/bhqk,bqhe->bkhe/dot_general | solution.py:66
  555.6 41.8 %fusion.69 = bf16[392,1,12,64]{0,3,2,1:T(8,128)(2,1)} fusion(f32[12,392,784]{2,1,0:T(8,128)} %fusion.66, f32[12,392,784]{2,1,0:T(8,128)} %get-tuple-element.41, f32[12,392]{1,0:T(8,128)S(1)} %log_add_fusion, bf16[784,1,12,64]{0,3,2,1:T(8,128)(2,1)} %copy.72), kind=kOutput, calls=%fused_computation.92 | convolution fusion | flops 498177920 | bytes 31328640 | tf_op jit(solution)/shard_map/bhqk,bkhe->bqhe/dot_general | solution.py:63
  604.2 6.8 fusion.58
  612.5 8.6 fusion.119
  622.2 9.6 fusion.114
  632.5 7.5 add_convert_fusion.3
  649.0 40.4 %all-reduce.4 = (f32[4,768]{1,0:T(4,128)S(1)}, f32[4,768]{1,0:T(4,128)S(1)}, f32[3072]{0:T(1024)S(1)}) all-reduce(f32[4,768]{1,0:T(4,128)S(1)} %pad_maximum_fusion.11, f32[4,768]{1,0:T(4,128)S(1)} %pad_maximum_fusion.12, f32[3072]{0:T(1024)S(1)} %get-tuple-element.50), channel_id=10, replica_groups=mesh['dp'=16,'seq'=2] {'dp','seq'}, use_global_device_ids=true, to_apply=%region_24.25.clone | all-reduce | flops 9216 | bytes 73728
  694.9 90.1 %reduce-scatter.13.cloned.1.call-done = f32[24,2304]{1,0:T(8,128)} async-done(((f32[768,2304]{1,0:T(8,128)}), f32[24,2304]{1,0:T(8,128)}) %reduce-scatter.13.cloned.1.call-update) | async-done | bytes 221200 | tf_op jit(solution)/shard_map/reduce_scatter | solution.py:197
  785.0 141.3 %reduce-scatter.17.cloned.1.call-done = f32[24,3072]{1,0:T(8,128)} async-done(((f32[768,3072]{1,0:T(8,128)}), f32[24,3072]{1,0:T(8,128)}) %reduce-scatter.17.cloned.1.call-update) | async-done | bytes 294928 | tf_op jit(solution)/shard_map/reduce_scatter | solution.py:199
  926.4 141.8 %reduce-scatter.19.cloned.1.call-done = f32[96,768]{1,0:T(8,128)} async-done(((f32[3072,768]{1,0:T(8,128)}), f32[96,768]{1,0:T(8,128)}) %reduce-scatter.19.cloned.1.call-update) | async-done | bytes 294928 | tf_op jit(solution)/shard_map/reduce_scatter | solution.py:200
  (198 shorter events, 113.3 us)
Async XLA Ops:
  7.2 140.8 %copy-start.6 = (bf16[1,392,768]{2,1,0:T(8,128)(2,1)S(1)}, bf16[1,392,768]{2,1,0:T(8,128)(2,1)}, u32[]{:S(2)}) copy-start(bf16[1,392,768]{2,1,0:T(8,128)(2,1)} %param.14) | copy-start | bytes 1806340
  7.2 140.8 %copy-start.10 = (bf16[1,196,768]{2,1,0:T(8,128)(2,1)S(1)}, bf16[1,196,768]{2,1,0:T(8,128)(2,1)}, u32[]{:S(2)}) copy-start(bf16[1,196,768]{2,1,0:T(8,128)(2,1)} %param.13) | copy-start | bytes 903172
  7.2 140.8 %all-gather.11.cloned.1.call-start = ((), (), s32[]{:S(2)}) async-start(), calls=%async_computation.6 | async-start | bytes 3649536 | tf_op jit(solution)/shard_map/all_gather | solution.py:86
  8.9 205.1 %all-gather.21.cloned.1.call-start = ((), (), s32[]{:S(2)}) async-start(), calls=%async_computation.15 | async-start | bytes 4816896 | tf_op jit(solution)/shard_map/all_gather | solution.py:121
  146.2 6.4 copy-start.30
  146.2 6.4 copy-start.35
  162.9 92.0 %all-gather.19.cloned.1.call-start = ((), (), s32[]{:S(2)}) async-start(), calls=%async_computation.14 | async-start | bytes 4816896 | tf_op jit(solution)/shard_map/all_gather | solution.py:122
  163.0 6.6 copy-start.40
  166.0 42.1 %slice-start = ((bf16[588,2304]{1,0:T(8,128)(2,1)}), bf16[196,2304]{1,0:T(8,128)(2,1)S(1)}, s32[]{:S(2)}) async-start(bf16[588,2304]{1,0:T(8,128)(2,1)} %copy-done.13), calls=%async_computation.18 | async-start | bytes 1843200 | tf_op jit(solution)/shard_map/slice | solution.py:113
  166.0 146.5 %all-gather.13.cloned.1.call-start = ((), (), s32[]{:S(2)}) async-start(), calls=%async_computation.7 | async-start | bytes 1216512 | tf_op jit(solution)/shard_map/all_gather | solution.py:87
  166.7 211.7 %all-gather.15.cloned.1.call-start = ((), (), s32[]{:S(2)}) async-start(), calls=%async_computation.8 | async-start | bytes 4866048 | tf_op jit(solution)/shard_map/all_gather | solution.py:88
  167.5 276.8 %all-gather.17.cloned.1.call-start = ((), (), s32[]{:S(2)}) async-start(), calls=%async_computation.9 | async-start | bytes 4866048 | tf_op jit(solution)/shard_map/all_gather | solution.py:89
  168.2 429.2 %reduce-scatter.23.cloned.1.call-start = ((), (), s32[]{:S(2)}) async-start(), calls=%async_computation.17 | async-start | bytes 1806336
  260.1 10.8 %copy-start = (f32[12,392,784]{2,1,0:T(8,128)S(1)}, f32[12,392,784]{2,1,0:T(8,128)}, u32[]{:S(2)}) copy-start(f32[12,392,784]{2,1,0:T(8,128)} %get-tuple-element.41) | copy-start | bytes 44255236
  444.2 10.2 copy-start.4
  444.2 10.2 copy-start.37
  478.6 120.2 %reduce-scatter.21.cloned.1.call-start = ((), (), s32[]{:S(2)}) async-start(), calls=%async_computation.16 | async-start | bytes 1806336
  533.7 161.2 %reduce-scatter.15.cloned.1.call-start = ((), (), s32[]{:S(2)}) async-start(), calls=%async_computation.11 | async-start | bytes 2433024 | tf_op jit(solution)/shard_map/reduce_scatter | solution.py:198
  537.8 247.2 %reduce-scatter.13.cloned.1.call-start = ((), (), s32[]{:S(2)}) async-start(), calls=%async_computation.10 | async-start | bytes 7299072 | tf_op jit(solution)/shard_map/reduce_scatter | solution.py:197
  555.6 47.2 %copy-start.11 = (bf16[1,196,3,12,64]{1,4,3,2,0:T(8,128)(2,1)}, bf16[1,196,3,12,64]{1,4,3,2,0:T(8,128)(2,1)S(1)}, u32[]{:S(2)}) copy-start(bf16[1,196,3,12,64]{1,4,3,2,0:T(8,128)(2,1)S(1)} %pad_maximum_fusion.4) | copy-start | bytes 2709508
  611.1 315.3 %reduce-scatter.17.cloned.1.call-start = ((), (), s32[]{:S(2)}) async-start(), calls=%async_computation.12 | async-start | bytes 9732096 | tf_op jit(solution)/shard_map/reduce_scatter | solution.py:199
  621.1 447.0 %reduce-scatter.19.cloned.1.call-start = ((), (), s32[]{:S(2)}) async-start(), calls=%async_computation.13 | async-start | bytes 9732096 | tf_op jit(solution)/shard_map/reduce_scatter | solution.py:200
  632.5 7.6 copy-start.9
  632.5 7.6 copy-start.12
  (30 other events, 76.6 us)
Sparse Core Ops, SparseCore 0:
  11.5 63.0 all-gather.10
  163.0 45.0 all-gather.20
  209.7 45.1 all-gather.18
  258.3 54.1 all-gather.12
  315.8 62.5 all-gather.14
  381.8 62.4 all-gather.16
  478.7 20.8 reduce-scatter.22
  533.8 20.9 reduce-scatter.20
  560.7 98.9 reduce-scatter.14
  666.7 118.2 reduce-scatter.12
  791.5 134.8 reduce-scatter.16
  933.7 134.3 reduce-scatter.18
where the time goes:
time: 1080 us
  waiting for transfers between devices  538 us (50%)
  matrix products  224 us (21%)
  blocking collectives  212 us (20%)
  local copies, waits for them, and re-layouts  57.9 us (5%)
  other arithmetic  26 us (2%)
  between operations  16.7 us (2%)
    reduce_scatter x1, waiting for transfers between devices, shards(): lax.psum_scatter(grad_down, ('dp', 'seq'), scatter_dimension=0, tiled=True)  142 us
    reduce_scatter x1, waiting for transfers between devices, shards(): lax.psum_scatter(grad_up, ('dp', 'seq'), scatter_dimension=0, tiled=True)  141 us
    reduce_scatter x1, waiting for transfers between devices, shards(): lax.psum_scatter(grad_qkv, ('dp', 'seq'), scatter_dimension=0, tiled=True)  90.1 us
    unnamed x2, blocking collectives  78.5 us
    all_gather x1, blocking collectives, shards(): lax.all_gather(proj_bias.astype(jnp.bfloat16), ('dp', 'seq'), axis=1, til...  69.8 us
    all_gather x1, blocking collectives, shards(): lax.all_gather(norm_params.astype(jnp.bfloat16), ('dp', 'seq'), axis=1, t...  63.4 us
    all_gather x1, waiting for transfers between devices, shards(): lax.all_gather(w_up.astype(jnp.bfloat16), ('dp', 'seq'), axis=0, tiled=True)  61.3 us
    dot_general x2, matrix products, attend_back(): jnp.einsum('bhqk,bqhe->bkhe', grad_raw, query, preferred_element_type=jnp...  47.1 us
  transfers between devices with their start and end apart: 12, of which 7 were waited for; matrix products, arithmetic and copies ran while one was open for 23% of the time, Pallas kernels for 0%

commit v1 on v0

--- a/solution.py
+++ b/solution.py
@@ -1,9 +1,894 @@
+import functools
+
 import jax
 import jax.numpy as jnp
 from jax import lax
+from jax.experimental import pallas as pl
+from jax.experimental.pallas import tpu as pltpu
 from jax.sharding import PartitionSpec as P
 
 HEAD_DIM = 64
+MESH = pl.DeviceIdType.MESH
+BF = jnp.bfloat16
+F32 = jnp.float32
+
+
+def dot(a, b):
+    return lax.dot_general(a, b, (((1,), (0,)), ((), ())), preferred_element_type=F32)
+
+
+def dot_rows(a, b):
+    return lax.dot_general(a, b, (((0,), (0,)), ((), ())), preferred_element_type=F32)
+
+
+def dot_cols(a, b):
+    return lax.dot_general(a, b, (((1,), (1,)), ((), ())), preferred_element_type=F32)
+
+
+def place():
+    d = lax.axis_index("dp")
+    return lax.axis_index("seq"), (d // 2) % 2, d // 4, d % 2
+
+
+def device(x, y, z, c):
+    return ((z * 2 + y) * 2 + c, x)
+
+
+def greet(partners):
+    bar = pltpu.get_barrier_semaphore()
+    for p in partners:
+        pl.semaphore_signal(bar, inc=1, device_id=p, device_id_type=MESH)
+    pl.semaphore_wait(bar, len(partners))
+
+
+def neighbours(x, y, z, c):
+    zs = [(z + k) % 4 for k in (1, 2, 3)]
+    return (
+        device(x, y, z, 1 - c),
+        device(1 - x, y, z, c),
+        device(x, 1 - y, z, c),
+        [device(x, y, k, c) for k in zs],
+        zs,
+    )
+
+
+def rcopy(src, dst, send, recv, dev):
+    return pltpu.make_async_remote_copy(
+        src_ref=src, dst_ref=dst, send_sem=send, recv_sem=recv, device_id=dev, device_id_type=MESH
+    )
+
+
+def stack_halves(g):
+    n = g.shape[1] // 2
+    return jnp.concatenate([g[:, :n], g[:, n:]], axis=0)
+
+
+def assemble(S, b, dst, col):
+    w, h = b // 2, b % 2
+    n = S.shape[-1]
+
+    def step(j, _):
+        z, y, c = j // 4, (j // 2) % 2, j % 2
+        a = S[w, h, 0, y, z, c].astype(F32)
+        e = S[w, h, 1, y, z, c].astype(F32)
+        k = a.shape[0] // 2
+        rows = pl.ds(pl.multiple_of(j * 2 * k, 16), 2 * k)
+        dst[rows, col : col + n] = jnp.concatenate([a[:k], e[:k]], axis=0).astype(BF)
+        dst[rows, col + n : col + 2 * n] = jnp.concatenate([a[k:], e[k:]], axis=0).astype(BF)
+        return 0
+
+    lax.fori_loop(0, 16, step, 0)
+
+
+def assemble_down(S, b, dst):
+    w, h = b // 2, b % 2
+    n = S.shape[-1]
+    half = (b - 8) // 2
+
+    def step(j, _):
+        z, y, c = j // 4, (j // 2) % 2, j % 2
+        for x in range(2):
+            rows = pl.ds(pl.multiple_of(96 * (2 * j + x) + 48 * half, 16), 48)
+            dst[rows, n * h : n * h + n] = S[w, h, x, y, z, c]
+        return 0
+
+    lax.fori_loop(0, 16, step, 0)
+
+
+def gather_kernel(
+    wqkv, wout, wup, wdown, small, tokens,
+    fqkv, fout, fup, fdown, fsmall, ptok,
+    own, S, mytok, sm, smland, smb, ss, rs, tsem, sms, smr,
+):
+    x, y, z, c = place()
+    sib, xn, yn, zn, zs = neighbours(x, y, z, c)
+    greet([sib, xn, yn] + zn)
+    width = tokens.shape[1]
+    nrow = tokens.shape[0]
+    mytok[0:nrow, :] = tokens[...]
+    mytok[nrow:, :] = jnp.zeros((mytok.shape[0] - nrow, width), BF)
+    tcp = rcopy(mytok, ptok, tsem.at[0], tsem.at[1], xn)
+    tcp.start()
+    blocks = [wqkv[:, k * width : (k + 1) * width] for k in range(3)]
+    blocks.append(wout[...])
+    blocks += [wup[:, k * width : (k + 1) * width] for k in range(4)]
+    for b, g in enumerate(blocks):
+        own[b // 2, b % 2] = stack_halves(g).astype(BF)
+    for b in range(8, 12):
+        half, h = (b - 8) // 2, b % 2
+        n = width // 2
+        own[b // 2, h] = wdown[48 * half : 48 * half + 48, h * n : h * n + n].astype(BF)
+    for w in range(6):
+        S[w, c, x, y, z, c] = own[w, c]
+    c0 = [rcopy(own.at[w, 1 - c], S.at[w, 1 - c, x, y, z, c], ss.at[w, 0], rs.at[w, 0], sib) for w in range(6)]
+    for cp in c0:
+        cp.start()
+    sm[...] = small[...].astype(BF)
+
+    def join(k, dev):
+        cp = rcopy(sm, smland.at[k], sms.at[k], smr.at[k], dev)
+        cp.start()
+        return cp
+
+    def joined(cps, ks):
+        for cp in cps:
+            cp.wait()
+        tot = sm[...].astype(F32)
+        for k in ks:
+            tot = tot + smland[k].astype(F32)
+        sm[...] = tot.astype(BF)
+
+    joined([join(0, sib)], [0])
+
+    def zcopy(w, i):
+        k = zs[i]
+        src = S.at[w, c, x, y, z]
+        return rcopy(src, src, ss.at[w, 1 + i], rs.at[w, 1 + i], zn[i])
+
+    def zwait(w, i):
+        dst = S.at[w, c, x, y, zs[i]]
+        return rcopy(dst, dst, ss.at[w, 1 + 2 - i], rs.at[w, 1 + 2 - i], zn[i])
+
+    def stage1(w):
+        c0[w].wait()
+        for i in range(3):
+            zcopy(w, i).start()
+
+    def stage2(w, start):
+        if start:
+            for i in range(3):
+                zcopy(w, i).wait_send()
+                zwait(w, i).wait_recv()
+        src = S.at[w, c, x, y]
+
+        def go(dev, dst):
+            if start:
+                rcopy(src, src, ss.at[w, 4], rs.at[w, 4], dev).start()
+            else:
+                cp = rcopy(src, dst, ss.at[w, 4], rs.at[w, 4], dev)
+                cp.wait_send()
+                cp.wait_recv()
+
+        pl.when(c == 0)(lambda: go(xn, S.at[w, c, 1 - x, y]))
+        pl.when(c == 1)(lambda: go(yn, S.at[w, c, x, 1 - y]))
+
+    def stage3(w, start):
+        if start:
+            stage2(w, False)
+
+        def go(dev, src, dst):
+            if start:
+                rcopy(src, src, ss.at[w, 5], rs.at[w, 5], dev).start()
+            else:
+                cp = rcopy(src, dst, ss.at[w, 5], rs.at[w, 5], dev)
+                cp.wait_send()
+                cp.wait_recv()
+
+        pl.when(c == 0)(lambda: go(yn, S.at[w, c, :, y], S.at[w, c, :, 1 - y]))
+        pl.when(c == 1)(lambda: go(xn, S.at[w, c, x], S.at[w, c, 1 - x]))
+
+    def share(w):
+        src = S.at[w, c]
+        return rcopy(src, src, ss.at[w, 6], rs.at[w, 6], sib)
+
+    def use(w):
+        cp = share(w)
+        cp.wait_send()
+        dst = S.at[w, 1 - c]
+        rcopy(dst, dst, ss.at[w, 6], rs.at[w, 6], sib).wait_recv()
+        for b in (2 * w, 2 * w + 1):
+            if b < 3:
+                assemble(S, b, fqkv, b * width)
+            elif b == 3:
+                assemble(S, b, fout, 0)
+            elif b < 8:
+                assemble(S, b, fup, (b - 4) * width)
+            else:
+                assemble_down(S, b, fdown)
+
+    for t in range(10):
+        if t < 6:
+            stage1(t)
+        if t == 0:
+            joined([join(1 + i, zn[i]) for i in range(3)], [1, 2, 3])
+        if t == 1:
+            joined([join(4, xn)], [4])
+        if t == 2:
+            joined([join(5, yn)], [5])
+            fsmall[...] = sm[...].astype(F32)
+        if 1 <= t < 7:
+            stage2(t - 1, True)
+        if 2 <= t < 8:
+            stage3(t - 2, True)
+        if 3 <= t < 9:
+            stage3(t - 3, False)
+            share(t - 3).start()
+        if t >= 4:
+            use(t - 4)
+    tcp.wait()
+
+
+def vm():
+    return pl.BlockSpec(memory_space=pltpu.VMEM)
+
+
+def params(cid=None, limit=62):
+    return pltpu.CompilerParams(
+        collective_id=cid, has_side_effects=cid is not None, vmem_limit_bytes=limit << 20
+    )
+
+
+def gather(wqkv, wout, wup, wdown, small, tokens):
+    D = wout.shape[1]
+    FF = wup.shape[1]
+    half = D // 2
+    rows = -(-tokens.shape[0] // 16) * 16
+    sds = jax.ShapeDtypeStruct
+    return pl.pallas_call(
+        gather_kernel,
+        out_shape=(
+            sds((D, 3 * D), BF), sds((D, D), BF), sds((D, FF), BF), sds((FF, D), BF),
+            sds(small.shape, F32), sds((rows, D), BF),
+        ),
+        in_specs=[vm()] * 6,
+        out_specs=(vm(),) * 6,
+        scratch_shapes=[
+            pltpu.VMEM((6, 2, 48, half), BF),
+            pltpu.VMEM((6, 2, 2, 2, 4, 2, 48, half), BF),
+            pltpu.VMEM((rows, D), BF),
+            pltpu.VMEM(small.shape, BF),
+            pltpu.VMEM((6,) + small.shape, BF),
+            pltpu.VMEM(small.shape, BF),
+            pltpu.SemaphoreType.DMA((6, 7)),
+            pltpu.SemaphoreType.DMA((6, 7)),
+            pltpu.SemaphoreType.DMA((2,)),
+            pltpu.SemaphoreType.DMA((6,)),
+            pltpu.SemaphoreType.DMA((6,)),
+        ],
+        compiler_params=params(1),
+        name="gather",
+    )(wqkv, wout, wup, wdown, small, tokens)
+
+
+def normalize(v):
+    centred = v - jnp.mean(v, -1, keepdims=True)
+    scale = lax.rsqrt(jnp.mean(centred * centred, -1, keepdims=True) + 1e-06)
+    return centred * scale, scale
+
+
+def norm_back(v, gain, grad):
+    unit, scale = normalize(v)
+    lifted = grad * gain
+    inner = jnp.mean(lifted * unit, -1, keepdims=True)
+    return scale * (lifted - jnp.mean(lifted, -1, keepdims=True) - unit * inner), unit
+
+
+def rows_of(i, size):
+    return pl.ds(pl.multiple_of(i * size, 16), size)
+
+
+def lanes_of(i, size, base=0):
+    return pl.ds(pl.multiple_of(base + i * size, 128), size)
+
+
+def gelu_pair(h):
+    p = 0.3275911 * 0.7071067811865476
+    a = abs(h)
+    t = 1.0 / (1.0 + p * a)
+    e = jnp.exp(-0.5 * h * h)
+    poly = ((((1.061405429 * t - 1.453152027) * t + 1.421413741) * t - 0.284496736) * t + 0.254829592) * t
+    q = 0.5 * poly * e
+    phi = jnp.where(h >= 0, 1.0 - q, q)
+    return h * phi, phi + h * e * 0.3989422804014327
+
+
+def head_masks(n):
+    lane = lax.broadcasted_iota(jnp.int32, (n, 128), 1)
+    return lane < 64
+
+
+def heads_forward(QKV, MIX, LSE, bias, q0, nq, k0, nk, qb, D):
+    lane = lax.broadcasted_iota(jnp.int32, (qb, 128), 1)
+    first = lane < 64
+
+    def pair(hp, _):
+        k = QKV[k0 : k0 + nk, lanes_of(hp, 128, D)]
+        v = QKV[k0 : k0 + nk, lanes_of(hp, 128, 2 * D)]
+
+        def block(i, _):
+            rows = pl.ds(pl.multiple_of(q0 + i * qb, 16), qb)
+            q = QKV[rows, lanes_of(hp, 128)] * jnp.asarray(HEAD_DIM**-0.5, BF)
+            outs = []
+            lrows = pl.ds(pl.multiple_of(i * qb, 16), qb)
+            logs = LSE[lrows, :]
+            for head in range(2):
+                keep = first if head == 0 else jnp.logical_not(first)
+                qm = jnp.where(keep, q, jnp.zeros_like(q))
+                s = dot_cols(qm, k) + bias
+                top = jnp.max(s, -1, keepdims=True)
+                e = jnp.exp(s - top)
+                total = jnp.sum(e, -1, keepdims=True)
+                pr = (e * (1.0 / total)).astype(BF)
+                outs.append(dot(pr, v))
+                logs = jnp.where(lane == 2 * hp + head, top + jnp.log(total), logs)
+            LSE[lrows, :] = logs
+            MIX[rows, lanes_of(hp, 128)] = jnp.where(first, outs[0], outs[1]).astype(BF)
+            return 0
+
+        lax.fori_loop(0, nq // qb, block, 0)
+        return 0
+
+    lax.fori_loop(0, D // 128, pair, 0)
+
+
+def heads_backward(QKV, DMIX, DQKV, LSE, DELTA, DS, KB, q0, nq, k0, nk, kb, D):
+    firstq = lax.broadcasted_iota(jnp.int32, (nq, 128), 1) < 64
+    firstk = lax.broadcasted_iota(jnp.int32, (kb, 128), 1) < 64
+
+    def pair(hp, _):
+        q = QKV[q0 : q0 + nq, lanes_of(hp, 128)] * jnp.asarray(HEAD_DIM**-0.5, BF)
+        dm = DMIX[q0 : q0 + nq, lanes_of(hp, 128)]
+        zero = jnp.zeros_like(q)
+        qs = [jnp.where(firstq, q, zero), jnp.where(firstq, zero, q)]
+        dms = [jnp.where(firstq, dm, zero), jnp.where(firstq, zero, dm)]
+        lses = [LSE[pl.ds(2 * hp + head, 1), :][:, :nq] for head in range(2)]
+        deltas = [DELTA[pl.ds(2 * hp + head, 1), :][:, :nq] for head in range(2)]
+
+        def block(i, _):
+            rows = pl.ds(pl.multiple_of(k0 + i * kb, 16), kb)
+            lrows = pl.ds(pl.multiple_of(i * kb, 16), kb)
+            k = QKV[rows, lanes_of(hp, 128, D)]
+            v = QKV[rows, lanes_of(hp, 128, 2 * D)]
+            bias = KB[lrows, :][:, :1]
+            dks, dvs = [], []
+            for head in range(2):
+                s = dot_cols(k, qs[head]) + bias
+                pr = jnp.exp(s - lses[head])
+                dvs.append(dot(pr.astype(BF), dm))
+                dp = dot_cols(v, dms[head])
+                ds = (pr * (dp - deltas[head])).astype(BF)
+                dks.append(dot(ds, q))
+                DS[head, lrows, :nq] = ds
+            DQKV[rows, lanes_of(hp, 128, D)] = jnp.where(firstk, dks[0], dks[1]).astype(BF)
+            DQKV[rows, lanes_of(hp, 128, 2 * D)] = jnp.where(firstk, dvs[0], dvs[1]).astype(BF)
+            return 0
+
+        lax.fori_loop(0, nk // kb, block, 0)
+        k = QKV[k0 : k0 + nk, lanes_of(hp, 128, D)]
+        outs = [dot_rows(DS[head, :nk, :nq], k) for head in range(2)]
+        DQKV[q0 : q0 + nq, lanes_of(hp, 128)] = (
+            jnp.where(firstq, outs[0], outs[1]) * HEAD_DIM**-0.5
+        ).astype(BF)
+        return 0
+
+    lax.fori_loop(0, D // 128, pair, 0)
+
+
+def outer(GB, A, B, a0, b0, n):
+    size = GB.shape[0] // 3
+
+    def step(i, _):
+        a = A[0:n, lanes_of(i, size, a0)]
+        GB[rows_of(i, size), :] = dot_rows(a, B[0:n, b0 : b0 + GB.shape[1]])
+        return 0
+
+    lax.fori_loop(0, 3, step, 0)
+
+
+def store_blocks(GB, P, b):
+    w, h = b // 2, b % 2
+
+    def step(j, _):
+        z, y, c = j // 4, (j // 2) % 2, j % 2
+        g = GB[pl.ds(pl.multiple_of(j * 48, 8), 48), :]
+        for x in range(2):
+            P[w, h, x, y, z, c] = stack_halves(g[24 * x : 24 * x + 24]).astype(BF)
+        return 0
+
+    lax.fori_loop(0, 16, step, 0)
+
+
+def store_down(GB, P, f):
+    def step(j, _):
+        y, c = j // 2, j % 2
+        for x in range(2):
+            for half in range(2):
+                g = GB[pl.ds(pl.multiple_of((2 * j + x) * 96 + 48 * half, 8), 48), :]
+                for h in range(2):
+                    n = P.shape[-1]
+                    P[4 + half, h, x, y, f, c] = g[:, h * n : h * n + n].astype(BF)
+        return 0
+
+    lax.fori_loop(0, 4, step, 0)
+
+
+def layer_kernel(
+    xs, xl, xp, cs, cl, counts, wqkv, wout, wup, wdown, sp,
+    outs, outl, P, DH1, MID, DH1P, SG,
+    X, DY, H1, QKV, MIX, H2, DH2, ACT, DHB, GB, DQKV, DML, DMIX,
+    LSES, LSEL, DELS, DELL, LSEST, LSELT, DELST, DELLT, DS, KBS, KBL,
+):
+    D = xs.shape[1]
+    ns, nl = xs.shape[0], xl.shape[0]
+    rs = -(-ns // 16) * 16
+    rl = -(-nl // 16) * 16
+    R = rs + rl
+    RK = R + rl
+    RB = 32
+    seq = lax.axis_index("seq")
+    zero = functools.partial(jnp.zeros, dtype=BF)
+    X[ns - ns % 16 : rs, :] = zero((rs - (ns - ns % 16), D))
+    X[R - 16 : R, :] = zero((16, D))
+    X[0:ns, :] = xs[...]
+    X[rs : rs + nl, :] = xl[...]
+    X[R:RK, :] = xp[...]
+    DY[ns - ns % 16 : rs, :] = zero((rs - (ns - ns % 16), D))
+    DY[R - 16 : R, :] = zero((16, D))
+    DY[0:ns, :] = cs[...]
+    DY[rs : rs + nl, :] = cl[...]
+    SG[...] = jnp.zeros(SG.shape, F32)
+
+    def norm_one(i, _):
+        rows = rows_of(i, 48)
+        unit, _ = normalize(X[rows, :].astype(F32))
+        H1[rows, :] = (unit * sp[0:1, :] + sp[1:2, :]).astype(BF)
+        return 0
+
+    lax.fori_loop(0, RK // 48, norm_one, 0)
+    third, half = RK // 3, R // 2
+
+    def project(i, _):
+        rows = rows_of(i, third)
+        h = H1[rows, :]
+        QKV[rows, 0:D] = (dot(h, wqkv[:, 0:D]) + sp[4:5, :]).astype(BF)
+        QKV[rows, D : 2 * D] = dot(h, wqkv[:, D : 2 * D]).astype(BF)
+        QKV[rows, 2 * D :] = (dot(h, wqkv[:, 2 * D :]) + sp[5:6, :]).astype(BF)
+        return 0
+
+    lax.fori_loop(0, 3, project, 0)
+
+    small_count = counts[0]
+    large_count = counts[1]
+    kj = lax.broadcasted_iota(jnp.int32, (1, rs), 1)
+    bias_small = jnp.where(kj < small_count, 0.0, -1e30)
+    kj = lax.broadcasted_iota(jnp.int32, (1, 2 * rl), 1)
+
+    def large_bias(kj):
+        mine = kj < rl
+        inside = jnp.where(mine, kj, kj - rl)
+        where = inside + jnp.where(mine, seq, 1 - seq) * nl
+        return jnp.where((inside < nl) & (where < large_count), 0.0, -1e30)
+
+    heads_forward(QKV, MIX, LSES, bias_small, 0, rs, 0, rs, rs, D)
+    heads_forward(QKV, MIX, LSEL, large_bias(kj), rs, rl, rs, 2 * rl, 80, D)
+
+    def project_out(i, _):
+        rows = rows_of(i, half)
+        MID[rows, :] = dot(MIX[rows, :], wout[...])
+        return 0
+
+    lax.fori_loop(0, 2, project_out, 0)
+
+    def norm_two(i, _):
+        rows = rows_of(i, RB)
+        middle = X[rows, :].astype(F32) + MID[rows, :] + sp[6:7, :]
+        MID[rows, :] = middle
+        unit, _ = normalize(middle)
+        H2[rows, :] = (unit * sp[2:3, :] + sp[3:4, :]).astype(BF)
+        DH1[rows, :] = middle + sp[7:8, :]
+        return 0
+
+    lax.fori_loop(0, R // RB, norm_two, 0)
+
+    DH2[...] = jnp.zeros(DH2.shape, F32)
+
+    def quarter(f, _):
+        fl = lanes_of(f, D)
+        fr = pl.ds(pl.multiple_of(f * D, 16), D)
+        ub = sp[pl.ds(8 + f, 1), :]
+
+        def part(i, tot):
+            rows = rows_of(i, half)
+            hidden = dot(H2[rows, :], wup[:, fl]) + ub
+            dact = dot_cols(DY[rows, :], wdown[fr, :])
+            act, slope = gelu_pair(hidden)
+            ACT[rows, :] = act.astype(BF)
+            dh = (dact * slope).astype(BF)
+            DHB[rows, :] = dh
+            return tot + jnp.sum(dh.astype(F32), 0, keepdims=True)
+
+        SG[pl.ds(8 + f, 1), :] = lax.fori_loop(0, 2, part, jnp.zeros((1, D), F32))
+
+        def gather_up(i, _):
+            rows = rows_of(i, half)
+            DH1[rows, :] += dot(ACT[rows, :], wdown[fr, :])
+            DH2[rows, :] += dot_cols(DHB[rows, :], wup[:, fl])
+            return 0
+
+        lax.fori_loop(0, 2, gather_up, 0)
+        outer(GB, ACT, DY, 0, 0, R)
+        store_down(GB, P, f)
+        outer(GB, H2, DHB, 0, 0, R)
+
+        def step(j, _):
+            z, y, c = j // 4, (j // 2) % 2, j % 2
+            g = GB[pl.ds(pl.multiple_of(j * 48, 8), 48), :]
+            for x in range(2):
+                P[2 + f // 2, f % 2, x, y, z, c] = stack_halves(g[24 * x : 24 * x + 24]).astype(BF)
+            return 0
+
+        lax.fori_loop(0, 16, step, 0)
+        return 0
+
+    lax.fori_loop(0, 4, quarter, 0)
+    outs[...] = DH1[0:ns, :].astype(BF)
+    outl[...] = DH1[rs : rs + nl, :].astype(BF)
+
+    def back_two(i, sums):
+        rows = rows_of(i, RB)
+        grad = DH2[rows, :]
+        dy = DY[rows, :].astype(F32)
+        dv, unit = norm_back(MID[rows, :], sp[2:3, :], grad)
+        dmid = dy + dv
+        MID[rows, :] = dmid
+        low = dmid.astype(BF)
+        DML[rows, :] = low
+        return (
+            sums[0] + jnp.sum(grad * unit, 0, keepdims=True),
+            sums[1] + jnp.sum(grad, 0, keepdims=True),
+            sums[2] + jnp.sum(low.astype(F32), 0, keepdims=True),
+            sums[3] + jnp.sum(dy, 0, keepdims=True),
+        )
+
+    z1 = jnp.zeros((1, D), F32)
+    sums = lax.fori_loop(0, R // RB, back_two, (z1, z1, z1, z1))
+    SG[2:3, :] = sums[0]
+    SG[3:4, :] = sums[1]
+    SG[6:7, :] = sums[2]
+    SG[7:8, :] = sums[3]
+
+    def back_out(i, _):
+        rows = rows_of(i, half)
+        DMIX[rows, :] = dot_cols(DML[rows, :], wout[...]).astype(BF)
+        return 0
+
+    lax.fori_loop(0, 2, back_out, 0)
+    outer(GB, MIX, DML, 0, 0, R)
+    store_blocks(GB, P, 3)
+
+    lane = lax.broadcasted_iota(jnp.int32, (16, 128), 1)
+
+    def deltas(base, out):
+        def step(i, _):
+            rows = pl.ds(pl.multiple_of(base + i * 16, 16), 16)
+            acc = jnp.zeros((16, 128), F32)
+            for hp in range(D // 128):
+                pr = DMIX[rows, hp * 128 : hp * 128 + 128].astype(F32) * MIX[
+                    rows, hp * 128 : hp * 128 + 128
+                ].astype(F32)
+                a = jnp.sum(jnp.where(lane < 64, pr, 0.0), -1, keepdims=True)
+                e = jnp.sum(jnp.where(lane < 64, 0.0, pr), -1, keepdims=True)
+                acc = jnp.where(lane == 2 * hp, a, jnp.where(lane == 2 * hp + 1, e, acc))
+            out[pl.ds(pl.multiple_of(i * 16, 16), 16), :] = acc
+            return 0
+
+        return step
+
+    lax.fori_loop(0, rs // 16, deltas(0, DELS), 0)
+    lax.fori_loop(0, rl // 16, deltas(rs, DELL), 0)
+    kj = lax.broadcasted_iota(jnp.int32, (rs, 128), 0)
+    KBS[...] = jnp.where(kj < small_count, 0.0, -1e30)
+    kj = lax.broadcasted_iota(jnp.int32, (2 * rl, 128), 0)
+    KBL[...] = large_bias(kj)
+    LSEST[...] = jnp.transpose(LSES[...])
+    DELST[...] = jnp.transpose(DELS[...])
+    LSELT[...] = jnp.transpose(LSEL[...])
+    DELLT[...] = jnp.transpose(DELL[...])
+    heads_backward(QKV, DMIX, DQKV, LSEST, DELST, DS, KBS, 0, rs, 0, rs, rs, D)
+    heads_backward(QKV, DMIX, DQKV, LSELT, DELLT, DS, KBL, rs, rl, rs, 2 * rl, 160, D)
+
+    outer(GB, H1, DQKV, 0, 0, R)
+    store_blocks(GB, P, 0)
+    outer(GB, H1, DQKV, 0, D, RK)
+    store_blocks(GB, P, 1)
+    outer(GB, H1, DQKV, 0, 2 * D, RK)
+    store_blocks(GB, P, 2)
+    def back_qkv(i, sums):
+        rows = rows_of(i, half)
+        DH1[rows, :] = dot_cols(DQKV[rows, :], wqkv[...])
+        return (
+            sums[0] + jnp.sum(DQKV[rows, 0:D].astype(F32), 0, keepdims=True),
+            sums[1] + jnp.sum(DQKV[rows, 2 * D :].astype(F32), 0, keepdims=True),
+        )
+
+    sums = lax.fori_loop(0, 2, back_qkv, (z1, z1))
+    SG[4:5, :] = sums[0]
+    SG[5:6, :] = sums[1] + jnp.sum(DQKV[R:RK, 2 * D :].astype(F32), 0, keepdims=True)
+    DH1P[...] = dot_cols(DQKV[R:RK, D:], wqkv[:, D:]).astype(BF)
+
+
+def scatter_kernel(
+    P, DH1, DMID, DH1P, xs, xl, sp, SG,
+    gqkv, gout, gup, gdown, dxs, dxl, SGO,
+    X, DX, LP, LC, LA, LB, LZ, T, LF, SM, SML, ss, rs, tsem, sms, smr,
+):
+    x, y, z, c = place()
+    sib, xn, yn, zn, zs = neighbours(x, y, z, c)
+    greet([sib, xn, yn] + zn)
+    D = xs.shape[1]
+    ns, nl = xs.shape[0], xl.shape[0]
+    r1 = -(-ns // 16) * 16
+    rl = -(-nl // 16) * 16
+    R = r1 + rl
+    tcp = rcopy(DH1P, LP, tsem.at[0], tsem.at[1], xn)
+    tcp.start()
+    order = [2, 3, 4, 5, 1, 0]
+
+    def add(dst, dsts, src, srcs, n):
+        def step(i, _):
+            d = dsts(i)
+            dst[d] = (dst[d].astype(F32) + src[srcs(i)].astype(F32)).astype(BF)
+            return 0
+
+        lax.fori_loop(0, n, step, 0)
+
+    def first(w, start):
+        cp = rcopy(P.at[w, 1 - c], LC.at[w], ss.at[w, 0], rs.at[w, 0], sib)
+        if start:
+            cp.start()
+            return
+        cp.wait()
+        idx = lambda i: (i // 16, (i // 8) % 2, (i // 2) % 4, i % 2)
+        add(LC, lambda i: (w,) + idx(i), P, lambda i: (w, c) + idx(i), 32)
+
+    def second(w, start):
+        def go(dev, src, kept):
+            cp = rcopy(src, LA.at[w], ss.at[w, 1], rs.at[w, 1], dev)
+            if start:
+                cp.start()
+                return
+            cp.wait()
+            idx = lambda i: (i // 8, (i // 2) % 4, i % 2)
+            add(LA, lambda i: (w,) + idx(i), LC, lambda i: (w,) + kept(idx(i)), 16)
+
+        pl.when(c == 0)(lambda: go(yn, LC.at[w, :, 1 - y], lambda i: (i[0], y, i[1], i[2])))
+        pl.when(c == 1)(lambda: go(xn, LC.at[w, 1 - x], lambda i: (x, i[0], i[1], i[2])))
+
+    def third(w, start):
+        def go(dev, other, kept):
+            cp = rcopy(LA.at[w, other], LB.at[w], ss.at[w, 2], rs.at[w, 2], dev)
+            if start:
+                cp.start()
+                return
+            cp.wait()
+            idx = lambda i: (i // 2, i % 2)
+            add(LB, lambda i: (w,) + idx(i), LA, lambda i: (w, kept) + idx(i), 8)
+
+        pl.when(c == 0)(lambda: go(xn, 1 - x, x))
+        pl.when(c == 1)(lambda: go(yn, 1 - y, y))
+
+    def fourth(w, start):
+        cps = [rcopy(LB.at[w, zs[i]], LZ.at[w, i], ss.at[w, 3 + i], rs.at[w, 3 + i], zn[i]) for i in range(3)]
+        if start:
+            for cp in cps:
+                cp.start()
+            return
+        for cp in cps:
+            cp.wait()
+        for k in range(2):
+            tot = LB[w, z, k].astype(F32)
+            for i in range(3):
+                tot = tot + LZ[w, i, k].astype(F32)
+            T[w, k] = tot
+
+    def fifth(w, start):
+        cp = rcopy(T.at[w, 1 - c], LF.at[w], ss.at[w, 6], rs.at[w, 6], sib)
+        if start:
+            cp.start()
+            return
+        cp.wait()
+        mine, other = T[w, c], LF[w]
+        n = mine.shape[1]
+        for h in range(2):
+            g = jnp.where(c == h, mine, other)
+            b = 2 * w + h
+            if b >= 8:
+                half = (b - 8) // 2
+                gdown[48 * half : 48 * half + 48, n * h : n * h + n] = g
+                continue
+            dst, col = (gqkv, b * D) if b < 3 else (gout, 0) if b == 3 else (gup, (b - 4) * D)
+            dst[:, col : col + n] = g[0:24]
+            dst[:, col + n : col + 2 * n] = g[24:48]
+
+    stages = [first, second, third, fourth, fifth]
+    for w in order:
+        first(w, True)
+
+    X[0:ns, :] = xs[...]
+    X[r1 : r1 + nl, :] = xl[...]
+    X[ns - ns % 16 : ns, :] = xs[ns - ns % 16 :, :]
+    tcp.wait()
+
+    def back_one(base, size, partner):
+        def step(i, sums):
+            rows = pl.ds(pl.multiple_of(base + i * size, 16), size)
+            grad = DH1[rows, :]
+            if partner:
+                grad = grad + LP[pl.ds(pl.multiple_of(i * size, 16), size), :].astype(F32)
+            dv, unit = norm_back(X[rows, :].astype(F32), sp[0:1, :], grad)
+            DX[rows, :] = (DMID[rows, :] + dv).astype(BF)
+            return (
+                sums[0] + jnp.sum(grad * unit, 0, keepdims=True),
+                sums[1] + jnp.sum(grad, 0, keepdims=True),
+            )
+
+        return step
+
+    z1 = jnp.zeros((1, D), F32)
+    sums = lax.fori_loop(0, r1 // 16, back_one(0, 16, False), (z1, z1))
+    sums = lax.fori_loop(0, rl // 16, back_one(r1, 16, True), sums)
+    dxs[...] = DX[0:ns, :]
+    dxl[...] = DX[r1 : r1 + nl, :]
+    SM[...] = SG[...]
+    SM[0:1, :] = sums[0]
+    SM[1:2, :] = sums[1]
+
+    def join(ks, devs):
+        cps = [rcopy(SM, SML.at[k], sms.at[k], smr.at[k], dev) for k, dev in zip(ks, devs)]
+        for cp in cps:
+            cp.start()
+        for cp in cps:
+            cp.wait()
+        tot = SM[...]
+        for k in ks:
+            tot = tot + SML[k]
+        SM[...] = tot
+
+    for t in range(10):
+        for s in range(5):
+            k = t - s
+            if 0 <= k < 6:
+                stages[s](order[k], False)
+                if s < 4:
+                    stages[s + 1](order[k], True)
+        if t == 0:
+            join([0], [sib])
+        if t == 1:
+            join([1], [xn])
+        if t == 2:
+            join([2], [yn])
+        if t == 3:
+            join([3, 4, 5], zn)
+            SGO[...] = SM[...]
+
+
+def layer(xs, xl, xp, cs, cl, counts, wqkv, wout, wup, wdown, sp):
+    D = xs.shape[1]
+    ns, nl = xs.shape[0], xl.shape[0]
+    rs = -(-ns // 16) * 16
+    rl = -(-nl // 16) * 16
+    R = rs + rl
+    RK = R + rl
+    sds = jax.ShapeDtypeStruct
+    smem = pl.BlockSpec(memory_space=pltpu.SMEM)
+    return pl.pallas_call(
+        layer_kernel,
+        out_shape=(
+            sds((ns, D), BF), sds((nl, D), BF), sds((6, 2, 2, 2, 4, 2, 48, D // 2), BF),
+            sds((R, D), F32), sds((R, D), F32), sds((rl, D), BF), sds((16, D), F32),
+        ),
+        in_specs=[vm()] * 5 + [smem] + [vm()] * 5,
+        out_specs=(vm(),) * 7,
+        scratch_shapes=[
+            pltpu.VMEM((RK, D), BF),
+            pltpu.VMEM((R, D), BF),
+            pltpu.VMEM((RK, D), BF),
+            pltpu.VMEM((RK, 3 * D), BF),
+            pltpu.VMEM((R, D), BF),
+            pltpu.VMEM((R, D), BF),
+            pltpu.VMEM((R, D), F32),
+            pltpu.VMEM((R, D), BF),
+            pltpu.VMEM((R, D), BF),
+            pltpu.VMEM((D, D), F32),
+            pltpu.VMEM((RK, 3 * D), BF),
+            pltpu.VMEM((R, D), BF),
+            pltpu.VMEM((R, D), BF),
+            pltpu.VMEM((256, 128), F32),
+            pltpu.VMEM((512, 128), F32),
+            pltpu.VMEM((256, 128), F32),
+            pltpu.VMEM((512, 128), F32),
+            pltpu.VMEM((128, 256), F32),
+            pltpu.VMEM((128, 512), F32),
+            pltpu.VMEM((128, 256), F32),
+            pltpu.VMEM((128, 512), F32),
+            pltpu.VMEM((2, 2 * rl, rl), BF),
+            pltpu.VMEM((rs, 128), F32),
+            pltpu.VMEM((2 * rl, 128), F32),
+        ],
+        compiler_params=params(None, 63),
+        name="layer",
+    )(xs, xl, xp, cs, cl, counts, wqkv, wout, wup, wdown, sp)
+
+
+def scatter(blocks, dh1, dmid, dh1p, xs, xl, sp, sg):
+    D = xs.shape[1]
+    n = D // 2
+    rl = dh1p.shape[0]
+    R = dh1.shape[0]
+    sds = jax.ShapeDtypeStruct
+    dma = pltpu.SemaphoreType.DMA
+    return pl.pallas_call(
+        scatter_kernel,
+        out_shape=(
+            sds((24, 3 * D), F32), sds((24, D), F32), sds((24, 4 * D), F32), sds((96, D), F32),
+            sds(xs.shape, BF), sds(xl.shape, BF), sds(sg.shape, F32),
+        ),
+        in_specs=[vm()] * 8,
+        out_specs=(vm(),) * 7,
+        scratch_shapes=[
+            pltpu.VMEM((R, D), BF),
+            pltpu.VMEM((R, D), BF),
+            pltpu.VMEM((rl, D), BF),
+            pltpu.VMEM((6, 2, 2, 4, 2, 48, n), BF),
+            pltpu.VMEM((6, 2, 4, 2, 48, n), BF),
+            pltpu.VMEM((6, 4, 2, 48, n), BF),
+            pltpu.VMEM((6, 3, 2, 48, n), BF),
+            pltpu.VMEM((6, 2, 48, n), F32),
+            pltpu.VMEM((6, 48, n), F32),
+            pltpu.VMEM(sg.shape, F32),
+            pltpu.VMEM((6,) + sg.shape, F32),
+            dma((6, 7)), dma((6, 7)), dma((2,)), dma((6,)), dma((6,)),
+        ],
+        compiler_params=params(2),
+        name="scatter",
+    )(blocks, dh1, dmid, dh1p, xs, xl, sp, sg)
+
+
+def shards(
+    small_tokens, large_tokens, small_counts, large_counts, small_cot, large_cot,
+    w_qkv, w_out, w_up, w_down, norm_params, proj_bias, up_bias,
+):
+    D = w_out.shape[1]
+    ns, nl = small_tokens.shape[1], large_tokens.shape[1]
+    me = lax.axis_index("dp") * 2 + lax.axis_index("seq")
+    low = lambda v: v.astype(BF).astype(F32)
+    k, m = norm_params.shape[1], up_bias.shape[0]
+    small = jnp.zeros((16, D), F32)
+    small = lax.dynamic_update_slice(small, jnp.concatenate([low(norm_params), low(proj_bias)]), (0, me * k))
+    small = lax.dynamic_update_slice(small, low(up_bias)[None], (8 + me * m // D, me * m % D))
+    xs, xl = small_tokens.reshape(ns, D), large_tokens.reshape(nl, D)
+    cs, cl = small_cot.reshape(ns, D), large_cot.reshape(nl, D)
+    counts = jnp.concatenate([small_counts, large_counts])
+    fqkv, fout, fup, fdown, sp, xp = gather(w_qkv, w_out, w_up, w_down, small, xl)
+    outs, outl, blocks, dh1, dmid, dh1p, sg = layer(xs, xl, xp, cs, cl, counts, fqkv, fout, fup, fdown, sp)
+    gqkv, gout, gup, gdown, dxs, dxl, sg = scatter(blocks, dh1, dmid, dh1p, xs, xl, sp, sg)
+    cols = lax.dynamic_slice(sg, (0, me * k), (8, k))
+    gub = lax.dynamic_slice(sg, (8 + me * m // D, me * m % D), (1, m))[0]
+    return (
+        outs.reshape(small_tokens.shape), outl.reshape(large_tokens.shape),
+        dxs.reshape(small_tokens.shape), dxl.reshape(large_tokens.shape),
+        gqkv, gout, gup, gdown, cols[0:4], cols[4:8], gub,
+    )
 
 
 def norm_rows(values, gain, shift):
@@ -17,13 +902,13 @@
     return jax.nn.gelu(values, approximate=False)
 
 
-def dot_rows(left, right):
+def general_rows(left, right):
     return lax.dot_general(
         left, right, (((0,), (0,)), ((), ())), preferred_element_type=jnp.float32
     )
 
 
-def dot_cols(left, right):
+def general_cols(left, right):
     return lax.dot_general(
         left, right, (((1,), (1,)), ((), ())), preferred_element_type=jnp.float32
     )
@@ -67,7 +952,7 @@
     return (grad_query, grad_key, grad_value)
 
 
-def shards(
+def shards_general(
     small_tokens,
     large_tokens,
     small_counts,
@@ -144,21 +1029,21 @@
         [small_cot.reshape(small_rows, width_dim), large_cot.reshape(half_len, width_dim)]
     )
     grad_rows_full = grad_rows.astype(jnp.float32)
-    grad_down = dot_rows(act_low, grad_rows)
+    grad_down = general_rows(act_low, grad_rows)
     grad_bias_down = jnp.sum(grad_rows, 0, dtype=jnp.float32)
-    grad_act = dot_cols(grad_rows, back_down)
+    grad_act = general_cols(grad_rows, back_down)
     (grad_hidden,) = gelu_back(grad_act)
     grad_hidden_low = grad_hidden.astype(jnp.bfloat16)
-    grad_up = dot_rows(normed_two, grad_hidden_low)
+    grad_up = general_rows(normed_two, grad_hidden_low)
     grad_up_bias = jnp.sum(grad_hidden_low, 0, dtype=jnp.float32)
-    grad_normed_two = dot_cols(grad_hidden_low, back_up)
+    grad_normed_two = general_cols(grad_hidden_low, back_up)
     grad_mid_norm, grad_gain_two, grad_shift_two = norm_two_back(grad_normed_two)
     grad_middle = grad_rows_full + grad_mid_norm
     grad_middle_low = grad_middle.astype(jnp.bfloat16)
-    grad_out = dot_rows(mixed, grad_middle_low)
+    grad_out = general_rows(mixed, grad_middle_low)
     grad_bias_out = jnp.sum(grad_middle_low, 0, dtype=jnp.float32)
     grad_mixed = (
-        dot_cols(grad_middle_low, back_out).astype(jnp.bfloat16).reshape(-1, head_count, HEAD_DIM)
+        general_cols(grad_middle_low, back_out).astype(jnp.bfloat16).reshape(-1, head_count, HEAD_DIM)
     )
     grad_mixed_small = grad_mixed[:small_rows].reshape(
         small_images, small_len, head_count, HEAD_DIM
@@ -183,10 +1068,10 @@
         half_len, 3 * width_dim
     )
     grad_qkv_low = jnp.concatenate([grad_qkv_small, grad_qkv_large]).astype(jnp.bfloat16)
-    grad_qkv = dot_rows(normed_one, grad_qkv_low)
+    grad_qkv = general_rows(normed_one, grad_qkv_low)
     grad_bias_query = jnp.sum(grad_qkv_low[:, :width_dim], 0, dtype=jnp.float32)
     grad_bias_value = jnp.sum(grad_qkv_low[:, 2 * width_dim :], 0, dtype=jnp.float32)
-    grad_normed_one = dot_cols(grad_qkv_low, back_qkv)
+    grad_normed_one = general_cols(grad_qkv_low, back_qkv)
     grad_in_norm, grad_gain_one, grad_shift_one = norm_one_back(grad_normed_one)
     grad_input = (grad_middle + grad_in_norm).astype(jnp.bfloat16)
     small_grad = grad_input[:small_rows].reshape(small_tokens.shape)
@@ -246,4 +1131,5 @@
         P(None, ("dp", "seq")),
         P(("dp", "seq")),
     )
-    return jax.shard_map(shards, mesh=mesh, in_specs=in_specs, out_specs=out_specs, check_vma=False)
+    body = shards if (mesh.shape["dp"], mesh.shape["seq"]) == (16, 2) else shards_general
+    return jax.shard_map(body, mesh=mesh, in_specs=in_specs, out_specs=out_specs, check_vma=False)

time: 1080 us -> 382 us (0.35)
  waiting for transfers between devices: 538 us -> 0 us
  Pallas kernels: 0 us -> 363 us
  matrix products: 224 us -> 0 us
  blocking collectives: 212 us -> 0 us
  local copies, waits for them, and re-layouts: 57.9 us -> 14.2 us
  other arithmetic: 26 us -> 2.62 us
  between operations: 16.7 us -> 2.03 us
    reduce_scatter x4 -> x0, waiting for transfers between devices: 373 us -> none  [the longest x1 142 us: shards(): lax.psum_scatter(grad_down, ('dp', 'seq'), scatter_dimension=0, tiled=True)]
    pallas_call x0 -> x3, Pallas kernels: none -> 363 us  [the longest x1 154 us: layer(): pl.pallas_call(layer_kernel, out_shape=(sds((ns, D), BF), sds((nl, D), BF...]
    dot_general x24 -> x0, matrix products: 224 us -> none  [the longest x2 47.1 us: attend_back(): jnp.einsum('bhqk,bqhe->bkhe', grad_raw, query, preferred_element_type=jnp...]
    all_gather x6 -> x0, waiting for transfers between devices: 165 us -> none  [the longest x1 61.3 us: shards(): lax.all_gather(w_up.astype(jnp.bfloat16), ('dp', 'seq'), axis=0, tiled=True)]
    all_gather x2 -> x0, blocking collectives: 133 us -> none  [the longest x1 69.8 us: shards(): lax.all_gather(proj_bias.astype(jnp.bfloat16), ('dp', 'seq'), axis=1, til...]
    unnamed x2 -> x0, blocking collectives: 78.5 us -> none
    slice x14 -> x1, local copies, waits for them, and re-layouts: 20.6 us -> 0.59 us  [shards(): cols[4:8]]
    reduce_sum x10 -> x0, other arithmetic: 18.8 us -> none  [the longest x2 9.31 us: attend(): totals = jnp.sum(expo_rows, -1, keepdims=True)]
  transfers between devices with their start and end apart: 12 -> 0, of which waited for: 7 -> 0; matrix products, arithmetic and copies ran while one was open for 23% -> 0% of each run, Pallas kernels for 0% -> 0%
where the time goes in v1:
time: 382 us
  Pallas kernels  363 us (95%)
  local copies, waits for them, and re-layouts  14.2 us (4%)
    pallas_call x1, Pallas kernels, layer(): pl.pallas_call(layer_kernel, out_shape=(sds((ns, D), BF), sds((nl, D), BF...  154 us
    pallas_call x1, Pallas kernels, scatter(): pl.pallas_call(scatter_kernel, out_shape=(sds((24, 3 * D), F32), sds((24,...  117 us
    pallas_call x1, Pallas kernels, gather(): pl.pallas_call(gather_kernel, out_shape=(sds((D, 3 * D), BF), sds((D, D),...  91.7 us
    unnamed x8, local copies, waits for them, and re-layouts  10.8 us

profile of v1, /device:TPU:0, one launch (start us, length us, event | category | flops | bytes accessed | tf_op | source)
XLA Modules:
  0.0 381.6 jit_solution(14818990836077058477)
XLA Ops:
  2.0 0.6 pad_add_fusion.counts
  2.6 0.7 bitcast_convert_fusion
  3.2 0.7 convert_element_type.12
  3.9 0.7 convert_element_type.13
  4.6 0.5 dynamic_update_slice.6
  5.1 0.2 dynamic_update_slice.7.small
  5.4 0.0 copy-start
  5.4 0.6 copy-done
  6.0 91.7 %gather.1 = (bf16[768,2304]{1,0:T(8,128)(2,1)}, bf16[768,768]{1,0:T(8,128)(2,1)}, bf16[768,3072]{1,0:T(8,128)(2,1)}, bf16[3072,768]{1,0:T(8,128)(2,1)}, f32[16,768]{1,0:T(8,128)}, /*index=5*/bf16[400,768]{1,0:T(8,128)(2,1)}) custom-call(f32[24,2304]{1,0:T(8,128)} %wqkv.1, f32[24,768]{1,0:T(8,128)} %wout.1, f32[24,3072]{1,0:T(8,128)} %wup.1, ...), custom_call_target="tpu_custom_call" | custom-call | tf_op jit(solution)/shard_map/gather/pallas_call | solution.py:247
  97.7 153.6 %layer.1 = (bf16[196,768]{1,0:T(8,128)(2,1)}, bf16[392,768]{1,0:T(8,128)(2,1)}, bf16[6,2,2,2,4,2,48,384]{7,6,5,4,3,2,1,0:T(8,128)(2,1)}, f32[608,768]{1,0:T(8,12...) custom-call(bf16[196,768]{1,0:T(8,128)(2,1)} %bitcast.16, bf16[392,768]{1,0:T(8,128)(2,1)} %bitcast.14, ...), custom_call_target="tpu_custom_call" | custom-call | tf_op jit(solution)/shard_map/layer/pallas_call | solution.py:794
  251.3 117.5 %scatter.1 = (f32[24,2304]{1,0:T(8,128)}, f32[24,768]{1,0:T(8,128)}, f32[24,3072]{1,0:T(8,128)}, f32[96,768]{1,0:T(8,128)}, bf16[196,768]{1,0:T(8,128)(2,1)}, /*...) custom-call(bf16[6,2,2,2,4,2,48,384]{7,6,5,4,3,2,1,0:T(8,128)(2,1)} %get-tuple-element.39.P, f32[608,768]{1,0:T(8,128)} %get-tuple-element.40.DH1, ...), custom_call_target="tpu_custom_call" | custom-call | tf_op jit(solution)/shard_map/scatter/pallas_call | solution.py:840
  368.8 1.3 dynamic-slice_bitcast_fusion
  370.1 0.8 constant_dynamic-slice_fusion
  370.8 0.6 fusion
  371.4 1.7 copy.34
  373.1 1.9 copy.35
  375.0 1.6 copy.36
  376.7 1.5 copy.37
  378.2 1.7 copy.38
  379.9 1.7 copy.39
  (2 shorter events, 0.0 us)
Async XLA Ops:
  5.4 0.6 copy-start
